TPU v7x, 32 devices: a whole 2x2x4 slice. The times are simulated.
32 devices in a mesh: groups: 2 (over y), blk: 16 (over z, x, core).
Axes of the slice: x: 2, y: 2, z: 4, core: 2. Of those that a mesh axis runs over, the one named last changes fastest.
Arguments:
- snapshots: bfloat16 [64, 64, 16, 128], P(None, ('groups', 'blk')), parts along dimension 1, may hold values from -200 to 200
- old_modes: bfloat16 [192, 64, 16, 128], P(None, ('groups', 'blk')), parts along dimension 1, may hold values from -60 to 60
- mode_scales: float32 [384], P('groups'), parts along dimension 0, may hold values from 0.3 to 3
- plane_counts: int32 [32], P(('groups', 'blk')), parts along dimension 0, may hold values from 1 to 2, 20 in all
- links: int32 [32, 2], P(('groups', 'blk')), parts along dimension 0, may hold values from 0 to 1, as said below
Outputs:
- new_modes: bfloat16 [256, 64, 16, 128], P(None, ('groups', 'blk')), parts along dimension 1
- factor: float32 [512, 256], P('groups'), parts along dimension 0
There are 2 independent parts, one for each index of `groups`. A program takes and returns all parts, laid end to end along the dimension named above; each array names one. Nothing has to cross between parts.
Inputs may be any that keep to these rules, and one draw needn't show every extreme that they name: links[b, 1] equals links[b + 1 mod 16, 0]; 1 joins two blocks, 0 is a wall.
All inputs are finite; a program needn't handle non-finite values. No bound on the sum of `plane_counts` on one device may be relied on, other than what follows from the above.
Results may differ from a plain program's by a relative error of at most 0.0095.
Values may be sent and summed in bfloat16 or wider, within the bound.
A program may use at most 128 MiB of HBM per device.

v0:
```python
import jax
import jax.numpy as jnp
from jax import lax
from jax.sharding import PartitionSpec as P


def with_halo(x, sides, width):
    for axis, dim in sides:
        peers, length = (lax.axis_size(axis), x.shape[dim])
        up = [(i, (i + 1) % peers) for i in range(peers)]
        down = [(j, i) for i, j in up]
        last = lax.slice_in_dim(x, length - width, length, axis=dim)
        leading = lax.slice_in_dim(x, 0, width, axis=dim)
        before = lax.ppermute(last, axis, up)
        after = lax.ppermute(leading, axis, down)
        x = jnp.concatenate([before, x, after], axis=dim)
    return x


def smooth_along(field, along):
    widths = [(0, 0)] * field.ndim
    widths[along] = (1, 1)
    padded = jnp.pad(field, widths)
    length = field.shape[along]
    lower = lax.slice_in_dim(padded, 0, length, axis=along)
    upper = lax.slice_in_dim(padded, 2, length + 2, axis=along)
    return 0.25 * lower + 0.5 * field + 0.25 * upper


def gram_term(left_rows, right_rows):
    return lax.dot_general(
        left_rows, right_rows, (((1,), (1,)), ((), ())), preferred_element_type=jnp.float32
    )


def exact_dot(left_mat, right_mat):
    return jnp.dot(left_mat, right_mat, precision=lax.Precision.HIGHEST)


def leaf_factor(matrix):
    order = matrix.shape[0]
    row_ids = lax.iota(jnp.int32, order)
    lower = jnp.zeros((order, order), jnp.float32)
    for column in range(order):
        residue = matrix[:, column] - exact_dot(lower, lower[column, :])
        pivot = jnp.sqrt(residue[column])
        lower = lower.at[:, column].set(jnp.where(row_ids >= column, residue / pivot, 0.0))
    inverse = jnp.zeros((order, order), jnp.float32)
    for row in range(order):
        target = jnp.zeros((order,), jnp.float32).at[row].set(1.0)
        solved = (target - exact_dot(lower[row, :], inverse)) / lower[row, row]
        inverse = inverse.at[row, :].set(solved)
    return (lower, inverse)


def lower_factor(matrix):
    order = matrix.shape[0]
    if order <= 8:
        return leaf_factor(matrix)
    half = order // 2
    lower_one, inverse_one = lower_factor(matrix[:half, :half])
    below = exact_dot(matrix[half:, :half], inverse_one.T)
    rest = matrix[half:, half:] - exact_dot(below, below.T)
    lower_two, inverse_two = lower_factor(rest)
    corner = -exact_dot(inverse_two, exact_dot(below, inverse_one))
    top_zero = jnp.zeros((half, order - half), jnp.float32)
    lower = jnp.concatenate(
        [
            jnp.concatenate([lower_one, top_zero], axis=1),
            jnp.concatenate([below, lower_two], axis=1),
        ],
        axis=0,
    )
    inverse = jnp.concatenate(
        [
            jnp.concatenate([inverse_one, top_zero], axis=1),
            jnp.concatenate([corner, inverse_two], axis=1),
        ],
        axis=0,
    )
    return (lower, inverse)


def shards(snapshots, old_modes, mode_scales, plane_counts, links):
    new_count, plane_slots, rows_y, rows_z = snapshots.shape
    keep_count = old_modes.shape[0]
    columns = new_count + keep_count
    plane_count = plane_counts[0]
    plane_ids = lax.iota(jnp.int32, plane_slots)
    alive_mask = (plane_ids < plane_count).astype(jnp.float32)[None, :, None, None]
    last_pick = (plane_ids == plane_count - 1).astype(jnp.float32)[None, :, None, None]
    masked = snapshots.astype(jnp.float32) * alive_mask
    first_plane = masked[:, 0]
    last_plane = jnp.sum(masked * last_pick, axis=1)
    edge_planes = jnp.stack([first_plane, last_plane], axis=1).astype(jnp.bfloat16)
    widened = with_halo(edge_planes, (("blk", 1),), 1)
    left_halo = widened[:, 0].astype(jnp.float32) * links[0, 0].astype(jnp.float32)
    right_halo = widened[:, 3].astype(jnp.float32) * links[0, 1].astype(jnp.float32)
    behind = jnp.concatenate([left_halo[:, None], masked[:, :-1]], axis=1)
    forward = jnp.concatenate([masked[:, 1:], jnp.zeros_like(masked[:, :1])], axis=1)
    forward = forward + last_pick * right_halo[:, None]
    along_planes = 0.25 * behind + 0.5 * masked + 0.25 * forward
    filtered = (smooth_along(smooth_along(along_planes, 2), 3) * alive_mask).astype(jnp.bfloat16)
    scaled = (mode_scales[:, None, None, None] * old_modes.astype(jnp.float32) * alive_mask).astype(
        jnp.bfloat16
    )
    stacked = jnp.concatenate([filtered, scaled], axis=0).reshape(
        columns, plane_slots * rows_y * rows_z
    )
    cell_total = lax.axis_size("blk") * stacked.shape[1]
    local_gram = gram_term(stacked, stacked)
    gram = lax.psum(local_gram, "blk") / cell_total
    lower, inverse_lower = lower_factor(gram)
    factor = lower.T
    inverse_high = inverse_lower.astype(jnp.bfloat16)
    inverse_low = (inverse_lower - inverse_high.astype(jnp.float32)).astype(jnp.bfloat16)
    result = jnp.dot(inverse_high, stacked, preferred_element_type=jnp.float32)
    result = result + jnp.dot(inverse_low, stacked, preferred_element_type=jnp.float32)
    return (result.reshape(columns, plane_slots, rows_y, rows_z).astype(jnp.bfloat16), factor)


def solution(mesh):
    return jax.shard_map(
        shards,
        mesh=mesh,
        in_specs=(
            P(None, ("groups", "blk"), None, None),
            P(None, ("groups", "blk"), None, None),
            P("groups"),
            P(("groups", "blk")),
            P(("groups", "blk"), None),
        ),
        out_specs=(P(None, ("groups", "blk"), None, None), P("groups", None)),
        check_vma=False,
    )
```

profile of v0, /device:TPU:1, one launch (start us, length us, event | category | flops | bytes accessed | tf_op | source)
XLA Modules:
  0.0 922.3 jit_solution(12888956410553050702)
XLA Ops:
  7.9 1.4 multiply_reduce_fusion
  9.5 2.6 collective-permute-start
  21.0 1.4 convolution_bitcast_fusion
  22.4 1.5 pad_maximum_fusion
  24.0 2.9 copy.589
  26.9 88.5 %all-reduce.131.cloned.1.call-done = f32[256,256]{1,0:T(8,128)} async-done(((f32[256,256]{1,0:T(8,128)}), f32[256,256]{1,0:T(8,128)}) %all-reduce.131.cloned.1.call-update) | async-done | bytes 262160 | tf_op jit(solution)/shard_map/psum | solution.py:112
  115.4 1.0 broadcast_multiply_fusion
  139.8 0.8 fusion.32
  161.9 0.8 fusion.54
  162.8 0.8 fusion.57
  163.6 0.8 fusion.60
  187.3 0.8 fusion.88
  188.1 0.8 fusion.91
  188.9 0.8 fusion.94
  212.1 0.8 fusion.119
  213.0 0.8 fusion.122
  213.8 0.8 fusion.125
  237.0 0.8 fusion.150
  238.6 0.8 fusion.156
  260.8 0.8 fusion.178
  287.0 0.8 fusion.215
  287.8 0.8 fusion.218
  311.8 0.8 fusion.246
  312.6 0.8 fusion.249
  336.5 0.8 fusion.274
  338.1 0.8 fusion.280
  360.3 0.8 fusion.302
  361.1 0.8 fusion.305
  385.7 0.8 fusion.336
  387.3 0.8 fusion.342
  411.2 0.8 fusion.370
  412.0 0.8 fusion.373
  435.2 0.8 fusion.398
  436.8 0.8 fusion.404
  459.1 0.8 fusion.426
  486.1 0.8 fusion.466
  511.1 0.8 fusion.497
  536.7 0.8 fusion.528
  558.8 0.8 fusion.550
  585.2 0.8 fusion.587
  586.1 0.8 fusion.590
  609.9 0.8 fusion.618
  610.7 0.8 fusion.621
  634.8 0.8 fusion.649
  635.6 0.8 fusion.652
  657.7 0.8 fusion.674
  659.4 0.8 fusion.680
  684.7 0.8 fusion.714
  708.3 0.8 fusion.739
  710.0 0.8 fusion.745
  733.5 0.8 fusion.770
  735.1 0.8 fusion.776
  757.3 0.8 fusion.798
  784.3 0.8 fusion.838
  808.9 0.8 fusion.869
  833.3 0.8 fusion.897
  834.1 0.8 fusion.900
  856.2 0.8 fusion.922
  857.9 0.8 fusion.928
  883.4 0.8 fusion.962
  907.2 0.8 fusion.987
  908.8 0.8 fusion.993
  910.0 0.8 copy.591
  913.4 1.8 copy.625
  (2212 shorter events, 597.8 us)
Async XLA Ops:
  7.2 4.9 copy-start.3
  7.2 108.2 %all-reduce.131.cloned.1.call-start = ((), (), s32[]{:S(2)}) async-start(), calls=%async_computation | async-start | bytes 524288 | tf_op jit(solution)/shard_map/psum | solution.py:112
  7.9 4.2 copy-start.1
  9.4 10.2 %collective-permute-start.1 = (bf16[64,1,16,128]{3,0,2,1:T(8,128)(2,1)S(1)}, bf16[64,1,16,128]{3,0,2,1:T(8,128)(2,1)S(1)}, u32[]{:S(2)}, u32[]{:S(2)}) collective-permute-start(bf16[64,1,16,128]{3,0,2,1:T(8,128)(2,1)S(1)} %slice.17541), channel_id=1, source_target_pairs={{1,0},{2,1},{3,2},{4,3},{5,4},{6,5},{7,6},{8,7},{9,8},{10,9},{11,1... | collective-permute-start | bytes 786440 | tf_op jit(solution)/shard_map/ppermute | solution.py:15
  9.5 3.5 copy-start.2
  9.5 10.2 %collective-permute-start = (bf16[64,1,16,128]{3,0,2,1:T(8,128)(2,1)S(1)}, bf16[64,1,16,128]{3,0,2,1:T(8,128)(2,1)S(1)}, u32[]{:S(2)}, u32[]{:S(2)}) collective-permute-start(bf16[64,1,16,128]{3,0,2,1:T(8,128)(2,1)S(1)} %bitcast.7046), channel_id=1, source_target_pairs={{0,1},{1,2},{2,3},{3,4},{4,5},{5,6},{6,7},{7,8},{8,9},{9,10},{10,1... | collective-permute-start | bytes 786440 | tf_op jit(solution)/shard_map/ppermute | solution.py:14
  12.9 6.8 copy-start
  23.9 110.4 %copy-start.11 = (f32[8]{0:T(128)S(1)}, f32[8]{0:T(128)}, u32[]{:S(2)}) copy-start(f32[8]{0:T(128)} %constant.13709.clone.1) | copy-start | bytes 100
  23.9 111.1 %copy-start.10 = (f32[8]{0:T(128)S(1)}, f32[8]{0:T(128)}, u32[]{:S(2)}) copy-start(f32[8]{0:T(128)} %constant.13724.clone.1) | copy-start | bytes 100
  23.9 111.9 %copy-start.9 = (f32[8]{0:T(128)S(1)}, f32[8]{0:T(128)}, u32[]{:S(2)}) copy-start(f32[8]{0:T(128)} %constant.13725.clone.1) | copy-start | bytes 100
  23.9 112.7 %copy-start.8 = (f32[8]{0:T(128)S(1)}, f32[8]{0:T(128)}, u32[]{:S(2)}) copy-start(f32[8]{0:T(128)} %constant.13726.clone.1) | copy-start | bytes 100
  24.0 113.5 %copy-start.7 = (f32[8]{0:T(128)S(1)}, f32[8]{0:T(128)}, u32[]{:S(2)}) copy-start(f32[8]{0:T(128)} %constant.13727.clone.1) | copy-start | bytes 100
  24.0 114.2 %copy-start.6 = (f32[8]{0:T(128)S(1)}, f32[8]{0:T(128)}, u32[]{:S(2)}) copy-start(f32[8]{0:T(128)} %constant.13728.clone.1) | copy-start | bytes 100
  24.0 115.0 %copy-start.5 = (f32[8]{0:T(128)S(1)}, f32[8]{0:T(128)}, u32[]{:S(2)}) copy-start(f32[8]{0:T(128)} %constant.13729.clone.1) | copy-start | bytes 100
  24.0 115.8 %copy-start.4 = (f32[8]{0:T(128)S(1)}, f32[8]{0:T(128)}, u32[]{:S(2)}) copy-start(f32[8]{0:T(128)} %constant.13730.clone.1) | copy-start | bytes 100
Sparse Core Ops, SparseCore 0:
  22.6 92.7 all-reduce.130
where the time goes:
time: 937 us; the launch traced here: 922 us
  matrix products  245 us (26%)
  local copies, waits for them, and re-layouts  242 us (26%)
  between operations  178 us (19%)
  other arithmetic  166 us (18%)
  waiting for transfers between devices  88.5 us (9%)
    dot_general x605, matrix products, exact_dot(): return jnp.dot(left_mat, right_mat, precision=lax.Precision.HIGHEST)  242 us
    another operation x423, other arithmetic  157 us
    slice x224, local copies, waits for them, and re-layouts, leaf_factor(): pivot = jnp.sqrt(residue[column])  134 us
    psum x1, waiting for transfers between devices, shards(): gram = lax.psum(local_gram, 'blk') / cell_total  88.5 us
    slice x64, local copies, waits for them, and re-layouts, leaf_factor(): solved = (target - exact_dot(lower[row, :], inverse)) / lower[row, row]  42.5 us
    scatter x256, local copies, waits for them, and re-layouts, leaf_factor(): lower.at[:, column].set(jnp.where(row_ids >= column, residue / pivot, 0.0))  21 us
    another operation x256, local copies, waits for them, and re-layouts  20.9 us
  transfers between devices with their start and end apart: 3, of which 1 were waited for; matrix products, arithmetic and copies ran while one was open for 1% of the time, Pallas kernels for 0%

commit v1 on v0

--- a/solution.py
+++ b/solution.py
@@ -109,7 +109,7 @@
     )
     cell_total = lax.axis_size("blk") * stacked.shape[1]
     local_gram = gram_term(stacked, stacked)
-    gram = lax.psum(local_gram, "blk") / cell_total
+    gram = jnp.sum(lax.all_gather(local_gram, "blk"), axis=0) / cell_total
     lower, inverse_lower = lower_factor(gram)
     factor = lower.T
     inverse_high = inverse_lower.astype(jnp.bfloat16)

time: 937 us -> 896 us (0.956)
  waiting for transfers between devices: 88.5 us -> 47.3 us
  local copies, waits for them, and re-layouts: 242 us -> 230 us
    psum x1 -> x0, waiting for transfers between devices: 88.5 us -> none  [shards(): gram = lax.psum(local_gram, 'blk') / cell_total]
    all_gather x0 -> x1, waiting for transfers between devices: none -> 44 us  [shards(): gram = jnp.sum(lax.all_gather(local_gram, 'blk'), axis=0) / cell_total]
    slice x32 -> x0, local copies, waits for them, and re-layouts: 10.9 us -> none  [leaf_factor(): residue = matrix[:, column] - exact_dot(lower, lower[column, :])]
  transfers between devices with their start and end apart: 3 -> 3, of which waited for: 1 -> 3; matrix products, arithmetic and copies ran while one was open for 1% -> 1% of each run, Pallas kernels for 0% -> 0%
where the time goes in v1:
time: 896 us; the launch traced here: 881 us
  matrix products  254 us (28%)
  local copies, waits for them, and re-layouts  230 us (26%)
  between operations  179 us (20%)
  other arithmetic  168 us (19%)
  waiting for transfers between devices  47.3 us (5%)
    dot_general x605, matrix products, exact_dot(): return jnp.dot(left_mat, right_mat, precision=lax.Precision.HIGHEST)  251 us
    another operation x423, other arithmetic  157 us
    slice x224, local copies, waits for them, and re-layouts, leaf_factor(): pivot = jnp.sqrt(residue[column])  134 us
    all_gather x1, waiting for transfers between devices, shards(): gram = jnp.sum(lax.all_gather(local_gram, 'blk'), axis=0) / cell_total  44 us
    slice x64, local copies, waits for them, and re-layouts, leaf_factor(): solved = (target - exact_dot(lower[row, :], inverse)) / lower[row, row]  42.3 us
    another operation x256, local copies, waits for them, and re-layouts  20.9 us
    scatter x256, local copies, waits for them, and re-layouts, leaf_factor(): lower.at[:, column].set(jnp.where(row_ids >= column, residue / pivot, 0.0))  20.2 us
  transfers between devices with their start and end apart: 3, of which 3 were waited for; matrix products, arithmetic and copies ran while one was open for 1% of the time, Pallas kernels for 0%

profile of v1, /device:TPU:1, one launch (start us, length us, event | category | flops | bytes accessed | tf_op | source)
XLA Modules:
  0.0 880.6 jit_solution(14115165442604494694)
XLA Ops:
  7.9 1.4 multiply_reduce_fusion
  9.5 2.6 collective-permute-start
  14.9 1.2 collective-permute-done.1
  16.1 2.1 collective-permute-done
  19.6 1.4 convolution_bitcast_fusion
  25.8 1.5 pad_maximum_fusion
  27.3 2.9 copy.790
  30.2 44.0 %all-gather.3.cloned.1.call-done = f32[4096,256]{1,0:T(8,128)} async-done(((f32[256,256]{1,0:T(8,128)}), f32[4096,256]{1,0:T(8,128)}) %all-gather.3.cloned.1.call-update) | async-done | bytes 4194320 | tf_op jit(solution)/shard_map/all_gather | solution.py:112
  74.2 2.5 reduce_sum.19
  121.4 0.8 fusion.51
  144.3 0.8 fusion.76
  146.7 0.8 fusion.85
  169.1 0.8 fusion.107
  171.5 0.8 fusion.116
  193.9 0.8 fusion.138
  196.3 0.8 fusion.147
  220.0 0.8 fusion.175
  242.9 0.8 fusion.200
  245.3 0.8 fusion.209
  267.7 0.8 fusion.231
  270.1 0.8 fusion.240
  292.9 0.8 fusion.262
  295.3 0.8 fusion.271
  319.1 0.8 fusion.299
  342.0 0.8 fusion.324
  344.4 0.8 fusion.333
  366.6 0.8 fusion.355
  369.0 0.8 fusion.364
  391.4 0.8 fusion.386
  393.8 0.8 fusion.395
  440.8 0.8 fusion.448
  443.2 0.8 fusion.457
  465.7 0.8 fusion.479
  468.1 0.8 fusion.488
  491.1 0.8 fusion.510
  493.5 0.8 fusion.519
  517.2 0.8 fusion.547
  540.1 0.8 fusion.572
  542.5 0.8 fusion.581
  564.9 0.8 fusion.603
  567.3 0.8 fusion.612
  589.7 0.8 fusion.634
  592.1 0.8 fusion.643
  615.8 0.8 fusion.671
  638.7 0.8 fusion.696
  641.1 0.8 fusion.705
  663.5 0.8 fusion.727
  665.9 0.8 fusion.736
  688.7 0.8 fusion.758
  691.1 0.8 fusion.767
  714.9 0.8 fusion.795
  737.7 0.8 fusion.820
  740.2 0.8 fusion.829
  762.4 0.8 fusion.851
  764.8 0.8 fusion.860
  787.3 0.8 fusion.882
  789.7 0.8 fusion.891
  813.7 0.8 fusion.919
  836.7 0.8 fusion.944
  839.1 0.8 fusion.953
  862.1 0.8 fusion.975
  864.5 0.8 fusion.984
  868.2 0.8 copy.792
  871.6 1.8 copy.795
  (2182 shorter events, 595.7 us)
Async XLA Ops:
  7.2 4.9 copy-start.3
  7.2 67.0 %all-gather.3.cloned.1.call-start = ((), (), s32[]{:S(2)}) async-start(), calls=%async_computation | async-start | bytes 4456448 | tf_op jit(solution)/shard_map/all_gather | solution.py:112
  7.9 4.2 copy-start.1
  9.4 6.7 collective-permute-start.1
  9.5 3.5 copy-start.2
  9.5 8.7 collective-permute-start
  12.9 5.4 copy-start
  74.2 20.4 %copy-start.11 = (f32[8]{0:T(128)S(1)}, f32[8]{0:T(128)}, u32[]{:S(2)}) copy-start(f32[8]{0:T(128)} %constant.13709.clone.1) | copy-start | bytes 100
  74.2 21.1 %copy-start.10 = (f32[8]{0:T(128)S(1)}, f32[8]{0:T(128)}, u32[]{:S(2)}) copy-start(f32[8]{0:T(128)} %constant.13724.clone.1) | copy-start | bytes 100
  74.2 21.9 %copy-start.9 = (f32[8]{0:T(128)S(1)}, f32[8]{0:T(128)}, u32[]{:S(2)}) copy-start(f32[8]{0:T(128)} %constant.13725.clone.1) | copy-start | bytes 100
  74.2 22.7 %copy-start.8 = (f32[8]{0:T(128)S(1)}, f32[8]{0:T(128)}, u32[]{:S(2)}) copy-start(f32[8]{0:T(128)} %constant.13726.clone.1) | copy-start | bytes 100
  74.2 23.5 %copy-start.7 = (f32[8]{0:T(128)S(1)}, f32[8]{0:T(128)}, u32[]{:S(2)}) copy-start(f32[8]{0:T(128)} %constant.13727.clone.1) | copy-start | bytes 100
  74.2 24.3 %copy-start.6 = (f32[8]{0:T(128)S(1)}, f32[8]{0:T(128)}, u32[]{:S(2)}) copy-start(f32[8]{0:T(128)} %constant.13728.clone.1) | copy-start | bytes 100
  74.2 25.1 %copy-start.5 = (f32[8]{0:T(128)S(1)}, f32[8]{0:T(128)}, u32[]{:S(2)}) copy-start(f32[8]{0:T(128)} %constant.13729.clone.1) | copy-start | bytes 100
  74.2 25.9 %copy-start.4 = (f32[8]{0:T(128)S(1)}, f32[8]{0:T(128)}, u32[]{:S(2)}) copy-start(f32[8]{0:T(128)} %constant.13730.clone.1) | copy-start | bytes 100
Sparse Core Ops, SparseCore 0:
  21.2 52.9 all-gather.2
